TPU v7x, 32 devices: a whole 2x2x4 slice. The times are simulated.
32 devices in a mesh: dp: 16 (over z, y, core), layer: 2 (over x).
Axes of the slice: x: 2, y: 2, z: 4, core: 2. Of those that a mesh axis runs over, the one named last changes fastest.
Arguments:
- query_inputs: bfloat16 [2, 16, 128, 4096], P('layer', 'dp'), may hold values from -6 to 6
- query_cotangents: bfloat16 [2, 16, 128, 4096], P('layer', 'dp'), may hold values from -6 to 6
- query_lengths: int32 [16], P('dp'), may hold values from 64 to 128, as said below
- proj_in: bfloat16 [2, 64, 4096], P('layer'), may hold values from -0.09375 to 0.09375
- proj_out: bfloat16 [2, 64, 4096], P('layer'), may hold values from -0.09375 to 0.09375
- out_factor: float32 [2, 64, 64], P('layer'), may hold values from -1 to 5, as said below
- in_factor: float32 [2, 64, 64], P('layer'), may hold values from -1 to 5, as said below
- train_grads: bfloat16 [2, 2048, 4096], P('layer', 'dp'), may hold values from -0.0009765625 to 0.0009765625
Outputs:
- scores: float32 [16, 2048], P('layer', 'dp')
Inputs may be any that keep to these rules, and one draw needn't show every extreme that they name: `query_lengths`: some query sequence has 128 valid tokens and some has 64. `out_factor`: each matrix is symmetric positive definite. `in_factor`: each matrix is symmetric positive definite.
All inputs are finite; a program needn't handle non-finite values.
Results may differ from a plain program's by a relative error of at most 0.0057.
Values may be sent and summed in bfloat16 or wider, within the bound.
A program may use at most 64 MiB of HBM per device.

v0:
```python
import jax
import jax.numpy as jnp
from jax import lax
from jax.sharding import PartitionSpec as P


def body(
    query_inputs,
    query_cotangents,
    query_lengths,
    proj_in,
    proj_out,
    out_factor,
    in_factor,
    train_grads,
):
    blocks, queries, length, width = query_inputs.shape
    factor_rank = proj_in.shape[1]
    slots = lax.broadcasted_iota(jnp.int32, (1, queries, length, 1), 2)
    valid = slots < query_lengths[None, :, None, None]
    out_side = jnp.einsum(
        "bqld,brd->bqlr", query_cotangents, proj_out, preferred_element_type=jnp.float32
    )
    out_side = jnp.where(valid, out_side, 0.0).astype(jnp.bfloat16)
    in_side = jnp.einsum(
        "bqld,brd->bqlr", query_inputs, proj_in, preferred_element_type=jnp.float32
    ).astype(jnp.bfloat16)
    query_gradient_rows = jnp.einsum(
        "bqlr,bqls->bqrs", out_side, in_side, preferred_element_type=jnp.float32
    ).astype(jnp.bfloat16)
    flat_query = query_gradient_rows.reshape(blocks, queries, factor_rank * factor_rank)
    flat_grads = lax.all_gather(flat_query, "dp", axis=1, tiled=True)
    row_count = flat_grads.shape[1]
    widened = flat_grads.reshape(blocks, row_count, factor_rank, factor_rank).astype(jnp.float32)
    left_projection = jnp.einsum(
        "brk,bnks->bnrs", out_factor, widened, precision=lax.Precision.HIGHEST
    )
    both_sides = jnp.einsum(
        "bnrs,bst->bnrt", left_projection, in_factor, precision=lax.Precision.HIGHEST
    )
    partial_scores = jnp.einsum(
        "bnk,btk->nt",
        both_sides.astype(jnp.bfloat16).reshape(blocks, row_count, factor_rank * factor_rank),
        train_grads,
        preferred_element_type=jnp.float32,
    )
    return lax.psum_scatter(partial_scores, "layer", scatter_dimension=0, tiled=True)


def solution(mesh):
    in_specs = (
        P("layer", "dp", None, None),
        P("layer", "dp", None, None),
        P("dp"),
        P("layer", None, None),
        P("layer", None, None),
        P("layer", None, None),
        P("layer", None, None),
        P("layer", "dp", None),
    )
    out_specs = P("layer", "dp")
    return jax.shard_map(body, mesh=mesh, in_specs=in_specs, out_specs=out_specs, check_vma=False)
```

profile of v0, /device:TPU:0, one launch (start us, length us, event | category | flops | bytes accessed | tf_op | source)
XLA Modules:
  0.0 38.4 jit_solution(4139004014464007155)
XLA Ops:
  0.0 0.0 copy-start
  0.0 0.0 copy-start.2
  0.8 0.4 %copy-done = bf16[1,1,128,4096]{3,2,1,0:T(8,128)(2,1)S(1)} copy-done((bf16[1,1,128,4096]{3,2,1,0:T(8,128)(2,1)S(1)}, bf16[1,1,128,4096]{3,2,1,0:T(8,128)(2,1)}, u32[]{:S(2)}) %copy-start) | copy-done | bytes 1048600
  1.2 0.0 copy-start.3
  1.2 1.6 %fusion = bf16[128,64]{0,1:T(8,128)(2,1)S(1)} fusion(bf16[1,1,128,4096]{3,2,1,0:T(8,128)(2,1)S(1)} %copy-done, bf16[1,64,4096]{2,1,0:T(8,128)(2,1)} %param.12, pred[128]{0:T(512)(128)(4,1)S(1)} %iota_compare_fusion), kind=kOutput, calls=%fused_computation.4 | convolution fusion | flops 67125248 | bytes 1589376 | tf_op jit(solution)/shard_map/bqld,brd->bqlr/dot_general | solution.py:21
  2.8 0.0 copy-done.2
  2.8 0.0 copy-done.3
  2.9 0.6 %convolution_convert_fusion.2 = bf16[64,64]{1,0:T(8,128)(2,1)S(1)} fusion(bf16[128,64]{0,1:T(8,128)(2,1)S(1)} %fusion, bf16[1,1,128,4096]{3,2,1,0:T(8,128)(2,1)S(1)} %copy-done.2, bf16[1,64,4096]{2,1,0:T(8,128)(2,1)S(1)} %copy-done.3), kind=kOutput, calls=%fused_computation.5 | convolution fusion | flops 68169728 | bytes 1597440 | tf_op jit(solution)/shard_map/bqlr,bqls->bqrs/dot_general | solution.py:28
  3.4 0.1 reshape.67
  3.5 23.8 %all_gather.3 = bf16[1,16,4096]{2,0,1:T(2,128)(2,1)S(1)} all-gather(bf16[1,1,4096]{2,0,1:T(2,128)(2,1)S(1)} %bitcast.39), channel_id=1, replica_groups=mesh['dp'=16,'layer'=2] {'dp'}, dimensions={1}, use_global_device_ids=true | all-gather | bytes 139264 | tf_op jit(solution)/shard_map/all_gather | solution.py:32
  27.3 0.7 %reduce = bf16[16,4096]{1,0:T(8,128)(2,1)S(1)} reduce(bf16[1,16,4096]{2,0,1:T(2,128)(2,1)S(1)} %all_gather.3, bf16[]{:T(256)} %constant.14), dimensions={0}, to_apply=%all_gather.3.reduce_sub_computation | reduce | bytes 262146 | tf_op jit(solution)/shard_map/all_gather | solution.py:32
  28.1 0.0 copy-start.4
  28.1 0.0 copy-start.5
  28.1 0.2 reshape.68
  28.3 0.5 %copy-done.4 = f32[1,64,64]{2,1,0:T(8,128)S(1)} copy-done((f32[1,64,64]{2,1,0:T(8,128)S(1)}, f32[1,64,64]{2,1,0:T(8,128)}, u32[]{:S(2)}) %copy-start.4) | copy-done | bytes 16408
  28.8 0.0 copy-start.1
  28.8 0.4 %convolution_bitcast_fusion = f32[16,64,64]{1,2,0:T(8,128)S(1)} fusion(bf16[16,64,64]{2,1,0:T(8,128)(2,1)S(1)} %reshape.68, f32[1,64,64]{2,1,0:T(8,128)S(1)} %copy-done.4), kind=kOutput, calls=%fused_computation | convolution fusion | flops 50331648 | bytes 409600 | tf_op jit(solution)/shard_map/brk,bnks->bnrs/dot_general | solution.py:35
  29.3 0.0 copy-done.5
  29.3 1.0 %convolution_convert_fusion = bf16[16,64,64]{2,1,0:T(8,128)(2,1)S(1)} fusion(f32[16,64,64]{1,2,0:T(8,128)S(1)} %convolution_bitcast_fusion, f32[1,64,64]{2,1,0:T(8,128)S(1)} %copy-done.5), kind=kOutput, calls=%fused_computation.1 | convolution fusion | flops 50397184 | bytes 409600 | tf_op jit(solution)/shard_map/bnrs,bst->bnrt/dot_general | solution.py:38
  30.3 0.3 reshape.72
  30.5 0.0 copy-done.1
  30.6 0.4 fusion.1
  30.9 5.0 %all-reduce = f32[16,128]{1,0:T(8,128)S(1)} all-reduce(f32[16,128]{1,0:T(8,128)S(1)} %fusion.1), channel_id=2, replica_groups=mesh['dp'=16,'layer'=2] {'layer'}, use_global_device_ids=true, to_apply=%region_0.1.clone | all-reduce | flops 2048 | bytes 16384
  35.9 0.0 copy-start.6
  35.9 0.7 %copy-done.6 = u32[32]{0:T(128)S(1)} copy-done((u32[32]{0:T(128)S(1)}, u32[32]{0:T(128)}, u32[]{:S(2)}) %copy-start.6) | copy-done | bytes 152
  36.6 0.6 %dynamic-slice = u32[1]{0:T(128)} dynamic-slice(u32[32]{0:T(128)S(1)} %copy-done.6, u32[]{:T(128)S(6)} %add.3), dynamic_slice_sizes={1} | dynamic-slice | bytes 12
  37.8 0.6 %constant_dynamic-slice_fusion = f32[8,128]{1,0:T(8,128)} fusion(f32[16,128]{1,0:T(8,128)S(1)} %all-reduce, u32[]{:T(128)S(6)} %multiply.1), kind=kLoop, calls=%fused_computation.14 | loop fusion | bytes 8196
  (1 shorter events, 0.0 us)
Async XLA Ops:
  0.0 1.2 %copy-start = (bf16[1,1,128,4096]{3,2,1,0:T(8,128)(2,1)S(1)}, bf16[1,1,128,4096]{3,2,1,0:T(8,128)(2,1)}, u32[]{:S(2)}) copy-start(bf16[1,1,128,4096]{3,2,1,0:T(8,128)(2,1)} %param.9) | copy-start | bytes 3145732
  0.0 2.8 %copy-start.2 = (bf16[1,1,128,4096]{3,2,1,0:T(8,128)(2,1)S(1)}, bf16[1,1,128,4096]{3,2,1,0:T(8,128)(2,1)}, u32[]{:S(2)}) copy-start(bf16[1,1,128,4096]{3,2,1,0:T(8,128)(2,1)} %param.8) | copy-start | bytes 3145732
  1.2 1.6 %copy-start.3 = (bf16[1,64,4096]{2,1,0:T(8,128)(2,1)S(1)}, bf16[1,64,4096]{2,1,0:T(8,128)(2,1)}, u32[]{:S(2)}) copy-start(bf16[1,64,4096]{2,1,0:T(8,128)(2,1)} %param.11) | copy-start | bytes 1572868
  28.1 0.8 %copy-start.4 = (f32[1,64,64]{2,1,0:T(8,128)S(1)}, f32[1,64,64]{2,1,0:T(8,128)}, u32[]{:S(2)}) copy-start(f32[1,64,64]{2,1,0:T(8,128)} %param.13) | copy-start | bytes 49156
  28.1 1.2 %copy-start.5 = (f32[1,64,64]{2,1,0:T(8,128)S(1)}, f32[1,64,64]{2,1,0:T(8,128)}, u32[]{:S(2)}) copy-start(f32[1,64,64]{2,1,0:T(8,128)} %param.14) | copy-start | bytes 49156
  28.8 1.7 %copy-start.1 = (bf16[1,128,4096]{2,1,0:T(8,128)(2,1)S(1)}, bf16[1,128,4096]{2,1,0:T(8,128)(2,1)}, u32[]{:S(2)}) copy-start(bf16[1,128,4096]{2,1,0:T(8,128)(2,1)} %param.15) | copy-start | bytes 3145732
  35.9 0.7 %copy-start.6 = (u32[32]{0:T(128)S(1)}, u32[32]{0:T(128)}, u32[]{:S(2)}) copy-start(u32[32]{0:T(128)} %constant.12) | copy-start | bytes 388
where the time goes:
time: 38.7 us; the launch traced here: 38.4 us
  blocking collectives  28.8 us (74%)
  matrix products  3.97 us (10%)
  local copies, waits for them, and re-layouts  3.37 us (9%)
  between operations  1.54 us (4%)
  other arithmetic  0.74 us (2%)
    all_gather x1, blocking collectives, body(): flat_grads = lax.all_gather(flat_query, 'dp', axis=1, tiled=True)  23.8 us
    unnamed x1, blocking collectives  4.99 us
    unnamed x16, local copies, waits for them, and re-layouts  2.77 us
    dot_general x1, matrix products, body(): jnp.einsum('bqld,brd->bqlr', query_cotangents, proj_out, preferred_elemen...  1.58 us
    dot_general x1, matrix products, body(): jnp.einsum('bnrs,bst->bnrt', left_projection, in_factor, precision=lax.Pr...  0.99 us

commit v1 on v0

v1 whole, which is shorter than its diff:
```python
import functools

import jax
import jax.numpy as jnp
from jax import lax
from jax.experimental import pallas as pl
from jax.experimental.pallas import tpu as pltpu
from jax.sharding import PartitionSpec as P

MESH = pl.DeviceIdType.MESH
F32 = jnp.float32
BF16 = jnp.bfloat16
NT = (((1,), (1,)), ((), ()))
CHUNKS = 4


def split(x):
    high = x.astype(BF16).astype(F32)
    return high, x - high


def dot_nt(a, b):
    return lax.dot_general(a, b, NT, preferred_element_type=F32)


def kernel(
    n,
    m,
    inputs_hbm,
    cotangents_hbm,
    lengths_hbm,
    proj_in_hbm,
    proj_out_hbm,
    out_factor_hbm,
    in_factor_hbm,
    train_hbm,
    out_ref,
    inputs,
    cotangents,
    length,
    proj_in,
    proj_out,
    out_factor,
    in_factor,
    train,
    weights,
    own,
    gathered,
    wide,
    partial,
    arrived,
    load_sem,
    small_sem,
    send_sem,
    recv_sem,
    layer_send_sem,
    layer_recv_sem,
):
    me = lax.axis_index("dp")
    layer = lax.axis_index("layer")
    tokens, width = inputs.shape
    rank = proj_in.shape[0]
    step = width // CHUNKS

    def load(sem, src, dst):
        copy = pltpu.make_async_copy(src, dst, sem)
        copy.start()
        return copy

    def columns(c):
        return pl.ds(c * step, step)

    out_loads = []
    in_loads = []
    for c in range(CHUNKS):
        out_loads.append(
            (
                load(load_sem.at[0, c], proj_out_hbm.at[0, :, columns(c)], proj_out.at[:, columns(c)]),
                load(load_sem.at[1, c], cotangents_hbm.at[0, 0, :, columns(c)], cotangents.at[:, columns(c)]),
            )
        )
    out_factor_load = load(small_sem.at[0], out_factor_hbm.at[0], out_factor)
    in_factor_load = load(small_sem.at[1], in_factor_hbm.at[0], in_factor)
    length_load = load(small_sem.at[2], lengths_hbm, length)
    for c in range(CHUNKS):
        in_loads.append(
            (
                load(load_sem.at[2, c], proj_in_hbm.at[0, :, columns(c)], proj_in.at[:, columns(c)]),
                load(load_sem.at[3, c], inputs_hbm.at[0, 0, :, columns(c)], inputs.at[:, columns(c)]),
            )
        )
    train_load = load(small_sem.at[3], train_hbm.at[0], train)

    barrier = pltpu.get_barrier_semaphore()
    peers = [lax.rem(me + k, n) for k in range(1, n)]
    layers = [lax.rem(layer + k, m) for k in range(1, m)]
    for peer in peers:
        pl.semaphore_signal(barrier, inc=1, device_id=(peer, layer), device_id_type=MESH)
    for other in layers:
        pl.semaphore_signal(barrier, inc=1, device_id=(me, other), device_id_type=MESH)

    out_factor_load.wait()
    in_factor_load.wait()
    half = rank // 2
    pair = 2 * rank
    factor_rows = jnp.concatenate(
        [out_factor[pl.ds(0, half, stride=2), :], out_factor[pl.ds(1, half, stride=2), :]], axis=1
    )
    left = jnp.concatenate(split(factor_rows), axis=1).astype(BF16)
    in_high, in_low = split(in_factor[...])
    none = jnp.zeros((rank, rank), F32)
    top = jnp.concatenate([in_high, none, in_low, none], axis=1)
    bottom = jnp.concatenate([none, in_high, none, in_low], axis=1)
    weights[...] = jnp.concatenate([top, bottom, top, bottom], axis=0).astype(BF16)

    def project(loads, proj, values):
        total = None
        for c in range(CHUNKS):
            for copy in loads[c]:
                copy.wait()
            term = dot_nt(proj[:, columns(c)], values[:, columns(c)])
            total = term if total is None else total + term
        return total

    out_side = project(out_loads, proj_out, cotangents)
    length_load.wait()
    slots = lax.broadcasted_iota(jnp.int32, (rank, tokens), 1)
    out_side = jnp.where(slots < length[0], out_side, 0.0)
    in_side = project(in_loads, proj_in, inputs)
    out_twice = jnp.concatenate([out_side, out_side], axis=0).astype(BF16)
    in_twice = jnp.concatenate([in_side, in_side], axis=0).astype(BF16)
    grads = dot_nt(out_twice, in_twice)
    rows = lax.broadcasted_iota(jnp.int32, (pair, pair), 0) < rank
    cols = lax.broadcasted_iota(jnp.int32, (pair, pair), 1) < rank
    grads = jnp.where(rows == cols, grads, 0.0).astype(BF16)
    projected = jnp.dot(left, jnp.concatenate([grads, grads], axis=0), preferred_element_type=F32)
    projected = jnp.concatenate(split(projected), axis=1).astype(BF16)
    both = jnp.dot(projected, weights[...], preferred_element_type=F32)
    own[...] = (both[:, :pair] + both[:, pair:]).astype(BF16)

    pl.semaphore_wait(barrier, n - 1 + m - 1)
    sends = []
    for k in range(1, n):
        copy = pltpu.make_async_remote_copy(
            src_ref=own,
            dst_ref=gathered.at[me],
            send_sem=send_sem.at[k],
            recv_sem=recv_sem.at[me],
            device_id=(peers[k - 1], layer),
            device_id_type=MESH,
        )
        copy.start()
        sends.append(copy)
    gathered[me] = own[...]
    train_load.wait()
    for k in range(1, n):
        source = lax.rem(me + n - k, n)
        pltpu.make_async_remote_copy(
            src_ref=own,
            dst_ref=gathered.at[source],
            send_sem=send_sem.at[k],
            recv_sem=recv_sem.at[source],
            device_id=(peers[k - 1], layer),
            device_id_type=MESH,
        ).wait_recv()

    wide[...] = gathered[...].astype(F32).reshape(wide.shape)
    conditioned = jnp.concatenate(
        [wide[pl.ds(j, n, stride=half), :] for j in range(half)], axis=1
    ).astype(BF16)
    scores = dot_nt(conditioned, train[...])
    partial[...] = scores.reshape(partial.shape)
    layer_sends = []
    for k in range(1, m):
        copy = pltpu.make_async_remote_copy(
            src_ref=partial.at[layers[k - 1]],
            dst_ref=arrived.at[k],
            send_sem=layer_send_sem.at[k],
            recv_sem=layer_recv_sem.at[k],
            device_id=(me, layers[k - 1]),
            device_id_type=MESH,
        )
        copy.start()
        layer_sends.append(copy)
    total = partial[layer]
    for copy in sends:
        copy.wait_send()
    for k in range(1, m):
        layer_sends[k - 1].wait_recv()
        total = total + arrived[k]
    out_ref[...] = total
    for copy in layer_sends:
        copy.wait_send()


def body(n, m, *args):
    inputs, _, lengths, proj_in, _, _, _, train = args
    _, _, tokens, width = inputs.shape
    rank = proj_in.shape[1]
    count = train.shape[1]
    rows = n // m
    half, pair = rank // 2, 2 * rank
    hbm = pl.BlockSpec(memory_space=pl.ANY)
    return pl.pallas_call(
        functools.partial(kernel, n, m),
        out_shape=jax.ShapeDtypeStruct((rows, count), F32),
        in_specs=[hbm] * len(args),
        out_specs=pl.BlockSpec(memory_space=pltpu.VMEM),
        scratch_shapes=[
            pltpu.VMEM((tokens, width), BF16),
            pltpu.VMEM((tokens, width), BF16),
            pltpu.SMEM((1,), jnp.int32),
            pltpu.VMEM((rank, width), BF16),
            pltpu.VMEM((rank, width), BF16),
            pltpu.VMEM((rank, rank), F32),
            pltpu.VMEM((rank, rank), F32),
            pltpu.VMEM((count, rank * rank), BF16),
            pltpu.VMEM((2 * pair, 2 * pair), BF16),
            pltpu.VMEM((half, pair), BF16),
            pltpu.VMEM((n, half, pair), BF16),
            pltpu.VMEM((n * half, pair), F32),
            pltpu.VMEM((m, rows, count), F32),
            pltpu.VMEM((m, rows, count), F32),
            pltpu.SemaphoreType.DMA((4, CHUNKS)),
            pltpu.SemaphoreType.DMA((4,)),
            pltpu.SemaphoreType.DMA((n,)),
            pltpu.SemaphoreType.DMA((n,)),
            pltpu.SemaphoreType.DMA((m,)),
            pltpu.SemaphoreType.DMA((m,)),
        ],
        compiler_params=pltpu.CompilerParams(
            collective_id=0, has_side_effects=True, vmem_limit_bytes=48 * 1024 * 1024
        ),
    )(*args)


def solution(mesh):
    n, m = mesh.shape["dp"], mesh.shape["layer"]
    in_specs = (
        P("layer", "dp", None, None),
        P("layer", "dp", None, None),
        P("dp"),
        P("layer", None, None),
        P("layer", None, None),
        P("layer", None, None),
        P("layer", None, None),
        P("layer", "dp", None),
    )
    return jax.shard_map(
        functools.partial(body, n, m),
        mesh=mesh,
        in_specs=in_specs,
        out_specs=P("layer", "dp"),
        check_vma=False,
    )
```

time: 38.7 us -> 23.6 us (0.61)
  blocking collectives: 28.8 us -> 0 us
  Pallas kernels: 0 us -> 14.6 us
  local copies, waits for them, and re-layouts: 3.37 us -> 7.86 us
  matrix products: 3.97 us -> 0 us
  between operations: 1.54 us -> 0.67 us
  other arithmetic: 0.74 us -> 0 us
    all_gather x1 -> x0, blocking collectives: 23.8 us -> none  [body(): flat_grads = lax.all_gather(flat_query, 'dp', axis=1, tiled=True)]
    pallas_call x0 -> x1, Pallas kernels: none -> 14.6 us  [body(): pl.pallas_call(functools.partial(kernel, n, m), out_shape=jax.ShapeDtypeS...]
    unnamed x16 -> x15, local copies, waits for them, and re-layouts: 2.77 us -> 7.86 us
    unnamed x1 -> x0, blocking collectives: 4.99 us -> none
    dot_general x5 -> x0, matrix products: 3.97 us -> none  [the longest x1 1.58 us: body(): jnp.einsum('bqld,brd->bqlr', query_cotangents, proj_out, preferred_elemen...]
    all_gather x1 -> x0, other arithmetic: 0.73 us -> none  [body(): flat_grads = lax.all_gather(flat_query, 'dp', axis=1, tiled=True)]
    another operation x2 -> x0, local copies, waits for them, and re-layouts: 0.51 us -> none
where the time goes in v1:
time: 23.6 us; the launch traced here: 23.2 us
  Pallas kernels  14.6 us (62%)
  local copies, waits for them, and re-layouts  7.86 us (33%)
  between operations  0.67 us (3%)
    pallas_call x1, Pallas kernels, body(): pl.pallas_call(functools.partial(kernel, n, m), out_shape=jax.ShapeDtypeS...  14.6 us
    unnamed x15, local copies, waits for them, and re-layouts  7.86 us

profile of v1, /device:TPU:0, one launch (start us, length us, event | category | flops | bytes accessed | tf_op | source)
XLA Modules:
  0.0 23.2 jit_solution(17938668638126149253)
XLA Ops:
  0.7 0.0 copy-start
  0.7 1.2 %copy-done = bf16[1,1,128,4096]{3,2,1,0:T(8,128)(2,1)S(1)} copy-done((bf16[1,1,128,4096]{3,2,1,0:T(8,128)(2,1)S(1)}, bf16[1,1,128,4096]{3,2,1,0:T(8,128)(2,1)}, u32[]{:S(2)}) %copy-start) | copy-done | bytes 1048600
  1.9 0.0 copy-start.1
  1.9 1.2 %copy-done.1 = bf16[1,1,128,4096]{3,2,1,0:T(8,128)(2,1)S(1)} copy-done((bf16[1,1,128,4096]{3,2,1,0:T(8,128)(2,1)S(1)}, bf16[1,1,128,4096]{3,2,1,0:T(8,128)(2,1)}, u32[]{:S(2)}) %copy-start.1) | copy-done | bytes 1048600
  3.1 0.0 copy-start.2
  3.1 1.2 %copy-done.2 = bf16[1,128,4096]{2,1,0:T(8,128)(2,1)S(1)} copy-done((bf16[1,128,4096]{2,1,0:T(8,128)(2,1)S(1)}, bf16[1,128,4096]{2,1,0:T(8,128)(2,1)}, u32[]{:S(2)}) %copy-start.2) | copy-done | bytes 1048600
  4.3 0.0 copy-start.3
  4.3 1.0 %copy-done.3 = bf16[1,64,4096]{2,1,0:T(8,128)(2,1)S(1)} copy-done((bf16[1,64,4096]{2,1,0:T(8,128)(2,1)S(1)}, bf16[1,64,4096]{2,1,0:T(8,128)(2,1)}, u32[]{:S(2)}) %copy-start.3) | copy-done | bytes 524312
  5.4 0.0 copy-start.4
  5.4 1.0 %copy-done.4 = bf16[1,64,4096]{2,1,0:T(8,128)(2,1)S(1)} copy-done((bf16[1,64,4096]{2,1,0:T(8,128)(2,1)S(1)}, bf16[1,64,4096]{2,1,0:T(8,128)(2,1)}, u32[]{:S(2)}) %copy-start.4) | copy-done | bytes 524312
  6.4 0.0 copy-start.5
  6.4 0.8 %copy-done.5 = f32[1,64,64]{2,1,0:T(8,128)S(1)} copy-done((f32[1,64,64]{2,1,0:T(8,128)S(1)}, f32[1,64,64]{2,1,0:T(8,128)}, u32[]{:S(2)}) %copy-start.5) | copy-done | bytes 16408
  7.2 0.0 copy-start.6
  7.2 0.8 %copy-done.6 = f32[1,64,64]{2,1,0:T(8,128)S(1)} copy-done((f32[1,64,64]{2,1,0:T(8,128)S(1)}, f32[1,64,64]{2,1,0:T(8,128)}, u32[]{:S(2)}) %copy-start.6) | copy-done | bytes 16408
  7.9 14.6 %shard_map.82 = f32[8,128]{1,0:T(8,128)S(1)} custom-call(bf16[1,1,128,4096]{3,2,1,0:T(8,128)(2,1)S(1)} %copy-done, bf16[1,1,128,4096]{3,2,1,0:T(8,128)(2,1)S(1)} %copy-done.1, s32[1]{0:T(128)S(6)} %copy.10.lengths_hbm, bf16[1,64,4096]{2,1,0:T(8,128)(2,1)S(1)} %copy-done.3, bf16[1,64,4096]{2,1,0:T(8,128)(2,1)S(1)} %copy-done.4, f32[1,64,64]{2,1,0:T(8,128)S(1)} %copy-done.5, ...), custom_call_target="tpu_custom_call" | custom-call | tf_op jit(solution)/shard_map/pallas_call | solution.py:204
  22.6 0.6 %copy.11 = f32[8,128]{1,0:T(8,128)} copy(f32[8,128]{1,0:T(8,128)S(1)} %shard_map.82) | data formatting | bytes 8192
Async XLA Ops:
  0.7 1.2 %copy-start = (bf16[1,1,128,4096]{3,2,1,0:T(8,128)(2,1)S(1)}, bf16[1,1,128,4096]{3,2,1,0:T(8,128)(2,1)}, u32[]{:S(2)}) copy-start(bf16[1,1,128,4096]{3,2,1,0:T(8,128)(2,1)} %inputs_hbm.1) | copy-start | bytes 3145732
  1.9 1.2 %copy-start.1 = (bf16[1,1,128,4096]{3,2,1,0:T(8,128)(2,1)S(1)}, bf16[1,1,128,4096]{3,2,1,0:T(8,128)(2,1)}, u32[]{:S(2)}) copy-start(bf16[1,1,128,4096]{3,2,1,0:T(8,128)(2,1)} %cotangents_hbm.1) | copy-start | bytes 3145732
  3.1 1.2 %copy-start.2 = (bf16[1,128,4096]{2,1,0:T(8,128)(2,1)S(1)}, bf16[1,128,4096]{2,1,0:T(8,128)(2,1)}, u32[]{:S(2)}) copy-start(bf16[1,128,4096]{2,1,0:T(8,128)(2,1)} %train_hbm.1) | copy-start | bytes 3145732
  4.3 1.0 %copy-start.3 = (bf16[1,64,4096]{2,1,0:T(8,128)(2,1)S(1)}, bf16[1,64,4096]{2,1,0:T(8,128)(2,1)}, u32[]{:S(2)}) copy-start(bf16[1,64,4096]{2,1,0:T(8,128)(2,1)} %proj_in_hbm.1) | copy-start | bytes 1572868
  5.4 1.0 %copy-start.4 = (bf16[1,64,4096]{2,1,0:T(8,128)(2,1)S(1)}, bf16[1,64,4096]{2,1,0:T(8,128)(2,1)}, u32[]{:S(2)}) copy-start(bf16[1,64,4096]{2,1,0:T(8,128)(2,1)} %proj_out_hbm.1) | copy-start | bytes 1572868
  6.4 0.8 %copy-start.5 = (f32[1,64,64]{2,1,0:T(8,128)S(1)}, f32[1,64,64]{2,1,0:T(8,128)}, u32[]{:S(2)}) copy-start(f32[1,64,64]{2,1,0:T(8,128)} %out_factor_hbm.1) | copy-start | bytes 49156
  7.2 0.8 %copy-start.6 = (f32[1,64,64]{2,1,0:T(8,128)S(1)}, f32[1,64,64]{2,1,0:T(8,128)}, u32[]{:S(2)}) copy-start(f32[1,64,64]{2,1,0:T(8,128)} %in_factor_hbm.1) | copy-start | bytes 49156

commit v2 on v1

--- a/solution.py
+++ b/solution.py
@@ -200,7 +200,7 @@
     count = train.shape[1]
     rows = n // m
     half, pair = rank // 2, 2 * rank
-    hbm = pl.BlockSpec(memory_space=pl.ANY)
+    hbm = pl.BlockSpec(memory_space=pltpu.HBM)
     return pl.pallas_call(
         functools.partial(kernel, n, m),
         out_shape=jax.ShapeDtypeStruct((rows, count), F32),
@@ -229,7 +229,7 @@
             pltpu.SemaphoreType.DMA((m,)),
         ],
         compiler_params=pltpu.CompilerParams(
-            collective_id=0, has_side_effects=True, vmem_limit_bytes=48 * 1024 * 1024
+            collective_id=0, has_side_effects=True, vmem_limit_bytes=63 * 1024 * 1024
         ),
     )(*args)
 

time: 23.6 us -> 18.3 us (0.78); the launches traced: 23.2 us -> 18.1 us
  local copies, waits for them, and re-layouts: 7.86 us -> 1.28 us
  Pallas kernels: 14.6 us -> 16.2 us
    unnamed x15 -> x1, local copies, waits for them, and re-layouts: 7.86 us -> 1.28 us
    pallas_call x1, Pallas kernels: 14.6 us -> 16.2 us  [body(): pl.pallas_call(functools.partial(kernel, n, m), out_shape=jax.ShapeDtypeS...]
where the time goes in v2:
time: 18.3 us; the launch traced here: 18.1 us
  Pallas kernels  16.2 us (89%)
  local copies, waits for them, and re-layouts  1.28 us (7%)
  between operations  0.66 us (4%)
    pallas_call x1, Pallas kernels, body(): pl.pallas_call(functools.partial(kernel, n, m), out_shape=jax.ShapeDtypeS...  16.2 us
    unnamed x1, local copies, waits for them, and re-layouts  1.28 us

profile of v2, /device:TPU:0, one launch (start us, length us, event | category | flops | bytes accessed | tf_op | source)
XLA Modules:
  0.0 18.1 jit_solution(170519119910514001)
XLA Ops:
  0.7 16.2 %shard_map.82 = f32[8,128]{1,0:T(8,128)} custom-call(bf16[1,1,128,4096]{3,2,1,0:T(8,128)(2,1)} %inputs_hbm.1, bf16[1,1,128,4096]{3,2,1,0:T(8,128)(2,1)} %cotangents_hbm.1, s32[1]{0:T(128)S(6)} %copy.10.lengths_hbm, bf16[1,64,4096]{2,1,0:T(8,128)(2,1)} %proj_in_hbm.1, bf16[1,64,4096]{2,1,0:T(8,128)(2,1)} %proj_out_hbm.1, f32[1,64,64]{2,1,0:T(8,128)} %out_factor_hbm.1, ...), custom_call_target="tpu_custom_call" | custom-call | tf_op jit(solution)/shard_map/pallas_call | solution.py:204
  16.8 1.3 %copy.11 = f32[8,128]{1,0:T(8,128)} copy(f32[8,128]{1,0:T(8,128)} %shard_map.82) | data formatting | bytes 8192

commit v3 on v2

--- a/solution.py
+++ b/solution.py
@@ -28,7 +28,7 @@
     m,
     inputs_hbm,
     cotangents_hbm,
-    lengths_hbm,
+    length,
     proj_in_hbm,
     proj_out_hbm,
     out_factor_hbm,
@@ -37,7 +37,6 @@
     out_ref,
     inputs,
     cotangents,
-    length,
     proj_in,
     proj_out,
     out_factor,
@@ -51,6 +50,7 @@
     arrived,
     load_sem,
     small_sem,
+    train_sem,
     send_sem,
     recv_sem,
     layer_send_sem,
@@ -81,7 +81,6 @@
         )
     out_factor_load = load(small_sem.at[0], out_factor_hbm.at[0], out_factor)
     in_factor_load = load(small_sem.at[1], in_factor_hbm.at[0], in_factor)
-    length_load = load(small_sem.at[2], lengths_hbm, length)
     for c in range(CHUNKS):
         in_loads.append(
             (
@@ -89,15 +88,17 @@
                 load(load_sem.at[3, c], inputs_hbm.at[0, 0, :, columns(c)], inputs.at[:, columns(c)]),
             )
         )
-    train_load = load(small_sem.at[3], train_hbm.at[0], train)
+    core = lax.rem(me, 2)
+    sibling = me + 1 - 2 * core
+    train_load = load(small_sem.at[2], train_hbm.at[0], train.at[core])
 
     barrier = pltpu.get_barrier_semaphore()
-    peers = [lax.rem(me + k, n) for k in range(1, n)]
+    peers = [lax.rem(me + 2 * k, n) for k in range(1, n // 2)]
     layers = [lax.rem(layer + k, m) for k in range(1, m)]
-    for peer in peers:
-        pl.semaphore_signal(barrier, inc=1, device_id=(peer, layer), device_id_type=MESH)
-    for other in layers:
-        pl.semaphore_signal(barrier, inc=1, device_id=(me, other), device_id_type=MESH)
+    partners = [(sibling, layer)] + [(dp, other) for other in layers for dp in (me, sibling)]
+    greeted = [(peer, layer) for peer in peers] + partners
+    for device in greeted:
+        pl.semaphore_signal(barrier, inc=1, device_id=device, device_id_type=MESH)
 
     out_factor_load.wait()
     in_factor_load.wait()
@@ -123,9 +124,18 @@
         return total
 
     out_side = project(out_loads, proj_out, cotangents)
-    length_load.wait()
     slots = lax.broadcasted_iota(jnp.int32, (rank, tokens), 1)
     out_side = jnp.where(slots < length[0], out_side, 0.0)
+    pl.semaphore_wait(barrier, len(greeted))
+    train_share = pltpu.make_async_remote_copy(
+        src_ref=train_hbm.at[0],
+        dst_ref=train.at[core],
+        send_sem=train_sem.at[0],
+        recv_sem=train_sem.at[1],
+        device_id=(sibling, layer),
+        device_id_type=MESH,
+    )
+    train_share.start()
     in_side = project(in_loads, proj_in, inputs)
     out_twice = jnp.concatenate([out_side, out_side], axis=0).astype(BF16)
     in_twice = jnp.concatenate([in_side, in_side], axis=0).astype(BF16)
@@ -138,63 +148,85 @@
     both = jnp.dot(projected, weights[...], preferred_element_type=F32)
     own[...] = (both[:, :pair] + both[:, pair:]).astype(BF16)
 
-    pl.semaphore_wait(barrier, n - 1 + m - 1)
+    place = me // 2
     sends = []
-    for k in range(1, n):
+    for k, peer in enumerate(peers):
         copy = pltpu.make_async_remote_copy(
             src_ref=own,
-            dst_ref=gathered.at[me],
+            dst_ref=gathered.at[place],
             send_sem=send_sem.at[k],
-            recv_sem=recv_sem.at[me],
-            device_id=(peers[k - 1], layer),
+            recv_sem=recv_sem.at[place],
+            device_id=(peer, layer),
             device_id_type=MESH,
         )
         copy.start()
         sends.append(copy)
-    gathered[me] = own[...]
+    gathered[place] = own[...]
     train_load.wait()
-    for k in range(1, n):
-        source = lax.rem(me + n - k, n)
+    pltpu.make_async_remote_copy(
+        src_ref=train_hbm.at[0],
+        dst_ref=train.at[1 - core],
+        send_sem=train_sem.at[0],
+        recv_sem=train_sem.at[1],
+        device_id=(sibling, layer),
+        device_id_type=MESH,
+    ).wait_recv()
+    for k, peer in enumerate(peers):
+        source = peer // 2
         pltpu.make_async_remote_copy(
             src_ref=own,
             dst_ref=gathered.at[source],
             send_sem=send_sem.at[k],
             recv_sem=recv_sem.at[source],
-            device_id=(peers[k - 1], layer),
+            device_id=(peer, layer),
             device_id_type=MESH,
         ).wait_recv()
 
     wide[...] = gathered[...].astype(F32).reshape(wide.shape)
     conditioned = jnp.concatenate(
-        [wide[pl.ds(j, n, stride=half), :] for j in range(half)], axis=1
+        [wide[pl.ds(j, n // 2, stride=half), :] for j in range(half)], axis=1
     ).astype(BF16)
-    scores = dot_nt(conditioned, train[...])
-    partial[...] = scores.reshape(partial.shape)
-    layer_sends = []
-    for k in range(1, m):
+    scores = dot_nt(conditioned, train[...].reshape(2 * train.shape[1], train.shape[2]))
+    _, _, rows, count = partial.shape
+    for other in range(m):
+        for c in range(2):
+            partial[other, c] = scores[other * rows : (other + 1) * rows, c * count : (c + 1) * count]
+    results = []
+    for k, (dp, other) in enumerate(partners):
         copy = pltpu.make_async_remote_copy(
-            src_ref=partial.at[layers[k - 1]],
-            dst_ref=arrived.at[k],
+            src_ref=partial.at[other, lax.rem(dp, 2)],
+            dst_ref=arrived.at[layer, core],
             send_sem=layer_send_sem.at[k],
-            recv_sem=layer_recv_sem.at[k],
-            device_id=(me, layers[k - 1]),
+            recv_sem=layer_recv_sem.at[layer, core],
+            device_id=(dp, other),
             device_id_type=MESH,
         )
         copy.start()
-        layer_sends.append(copy)
-    total = partial[layer]
+        results.append(copy)
+    arrived[layer, core] = partial[layer, core]
+    train_share.wait_send()
     for copy in sends:
         copy.wait_send()
-    for k in range(1, m):
-        layer_sends[k - 1].wait_recv()
-        total = total + arrived[k]
-    out_ref[...] = total
-    for copy in layer_sends:
+    for k, (dp, other) in enumerate(partners):
+        pltpu.make_async_remote_copy(
+            src_ref=partial.at[other, lax.rem(dp, 2)],
+            dst_ref=arrived.at[other, lax.rem(dp, 2)],
+            send_sem=layer_send_sem.at[k],
+            recv_sem=layer_recv_sem.at[other, lax.rem(dp, 2)],
+            device_id=(dp, other),
+            device_id_type=MESH,
+        ).wait_recv()
+    for c in range(2):
+        total = arrived[0, c]
+        for other in range(1, m):
+            total = total + arrived[other, c]
+        out_ref[pl.ds(c, rows, stride=2), :] = total
+    for copy in results:
         copy.wait_send()
 
 
 def body(n, m, *args):
-    inputs, _, lengths, proj_in, _, _, _, train = args
+    inputs, _, _, proj_in, _, _, _, train = args
     _, _, tokens, width = inputs.shape
     rank = proj_in.shape[1]
     count = train.shape[1]
@@ -204,32 +236,32 @@
     return pl.pallas_call(
         functools.partial(kernel, n, m),
         out_shape=jax.ShapeDtypeStruct((rows, count), F32),
-        in_specs=[hbm] * len(args),
+        in_specs=[hbm, hbm, pl.BlockSpec(memory_space=pltpu.SMEM)] + [hbm] * 5,
         out_specs=pl.BlockSpec(memory_space=pltpu.VMEM),
         scratch_shapes=[
             pltpu.VMEM((tokens, width), BF16),
             pltpu.VMEM((tokens, width), BF16),
-            pltpu.SMEM((1,), jnp.int32),
             pltpu.VMEM((rank, width), BF16),
             pltpu.VMEM((rank, width), BF16),
             pltpu.VMEM((rank, rank), F32),
             pltpu.VMEM((rank, rank), F32),
-            pltpu.VMEM((count, rank * rank), BF16),
+            pltpu.VMEM((2, count, rank * rank), BF16),
             pltpu.VMEM((2 * pair, 2 * pair), BF16),
             pltpu.VMEM((half, pair), BF16),
-            pltpu.VMEM((n, half, pair), BF16),
-            pltpu.VMEM((n * half, pair), F32),
-            pltpu.VMEM((m, rows, count), F32),
-            pltpu.VMEM((m, rows, count), F32),
+            pltpu.VMEM((n // 2, half, pair), BF16),
+            pltpu.VMEM((n // 2 * half, pair), F32),
+            pltpu.VMEM((m, 2, rows // 2, count), F32),
+            pltpu.VMEM((m, 2, rows // 2, count), F32),
             pltpu.SemaphoreType.DMA((4, CHUNKS)),
-            pltpu.SemaphoreType.DMA((4,)),
-            pltpu.SemaphoreType.DMA((n,)),
-            pltpu.SemaphoreType.DMA((n,)),
-            pltpu.SemaphoreType.DMA((m,)),
-            pltpu.SemaphoreType.DMA((m,)),
+            pltpu.SemaphoreType.DMA((3,)),
+            pltpu.SemaphoreType.DMA((2,)),
+            pltpu.SemaphoreType.DMA((n // 2,)),
+            pltpu.SemaphoreType.DMA((n // 2,)),
+            pltpu.SemaphoreType.DMA((2 * m,)),
+            pltpu.SemaphoreType.DMA((m, 2)),
         ],
         compiler_params=pltpu.CompilerParams(
-            collective_id=0, has_side_effects=True, vmem_limit_bytes=63 * 1024 * 1024
+            collective_id=0, has_side_effects=True, vmem_limit_bytes=55212 * 1024
         ),
     )(*args)
 

time: 18.3 us -> 16.8 us (0.918)
  Pallas kernels: 16.2 us -> 15.4 us
  local copies, waits for them, and re-layouts: 1.28 us -> 0.6 us
    pallas_call x1, Pallas kernels: 16.2 us -> 15.4 us  [body(): pl.pallas_call(functools.partial(kernel, n, m), out_shape=jax.ShapeDtypeS...]
    unnamed x1, local copies, waits for them, and re-layouts: 1.28 us -> 0.6 us
where the time goes in v3:
time: 16.8 us; the launch traced here: 16.6 us
  Pallas kernels  15.4 us (92%)
  between operations  0.66 us (4%)
  local copies, waits for them, and re-layouts  0.6 us (4%)
    pallas_call x1, Pallas kernels, body(): pl.pallas_call(functools.partial(kernel, n, m), out_shape=jax.ShapeDtypeS...  15.4 us
    unnamed x1, local copies, waits for them, and re-layouts  0.6 us

profile of v3, /device:TPU:0, one launch (start us, length us, event | category | flops | bytes accessed | tf_op | source)
XLA Modules:
  0.0 16.6 jit_solution(10447339806651504615)
XLA Ops:
  0.7 15.4 %shard_map.82 = f32[8,128]{1,0:T(8,128)S(1)} custom-call(bf16[1,1,128,4096]{3,2,1,0:T(8,128)(2,1)} %inputs_hbm.1, bf16[1,1,128,4096]{3,2,1,0:T(8,128)(2,1)} %cotangents_hbm.1, s32[1]{0:T(128)S(6)} %copy.10.length, bf16[1,64,4096]{2,1,0:T(8,128)(2,1)} %proj_in_hbm.1, bf16[1,64,4096]{2,1,0:T(8,128)(2,1)} %proj_out_hbm.1, f32[1,64,64]{2,1,0:T(8,128)} %out_factor_hbm.1, ...), custom_call_target="tpu_custom_call" | custom-call | tf_op jit(solution)/shard_map/pallas_call | solution.py:236
  16.0 0.6 %copy.11 = f32[8,128]{1,0:T(8,128)} copy(f32[8,128]{1,0:T(8,128)S(1)} %shard_map.82) | data formatting | bytes 8192

commit v4 on v3

--- a/solution.py
+++ b/solution.py
@@ -11,7 +11,7 @@
 F32 = jnp.float32
 BF16 = jnp.bfloat16
 NT = (((1,), (1,)), ((), ()))
-CHUNKS = 4
+CHUNKS = 1
 
 
 def split(x):
@@ -100,6 +100,16 @@
     for device in greeted:
         pl.semaphore_signal(barrier, inc=1, device_id=device, device_id_type=MESH)
 
+    pl.semaphore_wait(barrier, len(greeted))
+    train_share = pltpu.make_async_remote_copy(
+        src_ref=train_hbm.at[0],
+        dst_ref=train.at[core],
+        send_sem=train_sem.at[0],
+        recv_sem=train_sem.at[1],
+        device_id=(sibling, layer),
+        device_id_type=MESH,
+    )
+    train_share.start()
     out_factor_load.wait()
     in_factor_load.wait()
     half = rank // 2
@@ -126,16 +136,6 @@
     out_side = project(out_loads, proj_out, cotangents)
     slots = lax.broadcasted_iota(jnp.int32, (rank, tokens), 1)
     out_side = jnp.where(slots < length[0], out_side, 0.0)
-    pl.semaphore_wait(barrier, len(greeted))
-    train_share = pltpu.make_async_remote_copy(
-        src_ref=train_hbm.at[0],
-        dst_ref=train.at[core],
-        send_sem=train_sem.at[0],
-        recv_sem=train_sem.at[1],
-        device_id=(sibling, layer),
-        device_id_type=MESH,
-    )
-    train_share.start()
     in_side = project(in_loads, proj_in, inputs)
     out_twice = jnp.concatenate([out_side, out_side], axis=0).astype(BF16)
     in_twice = jnp.concatenate([in_side, in_side], axis=0).astype(BF16)

time: 16.8 us -> 16.2 us (0.964)
  Pallas kernels: 15.4 us -> 14.8 us
    pallas_call x1, Pallas kernels: 15.4 us -> 14.8 us  [body(): pl.pallas_call(functools.partial(kernel, n, m), out_shape=jax.ShapeDtypeS...]
where the time goes in v4:
time: 16.2 us; the launch traced here: 16 us
  Pallas kernels  14.8 us (91%)
  between operations  0.66 us (4%)
  local copies, waits for them, and re-layouts  0.6 us (4%)
    pallas_call x1, Pallas kernels, body(): pl.pallas_call(functools.partial(kernel, n, m), out_shape=jax.ShapeDtypeS...  14.8 us
    unnamed x1, local copies, waits for them, and re-layouts  0.6 us

profile of v4, /device:TPU:0, one launch (start us, length us, event | category | flops | bytes accessed | tf_op | source)
XLA Modules:
  0.0 16.0 jit_solution(3839572482061209761)
XLA Ops:
  0.7 14.8 %shard_map.82 = f32[8,128]{1,0:T(8,128)S(1)} custom-call(bf16[1,1,128,4096]{3,2,1,0:T(8,128)(2,1)} %inputs_hbm.1, bf16[1,1,128,4096]{3,2,1,0:T(8,128)(2,1)} %cotangents_hbm.1, s32[1]{0:T(128)S(6)} %copy.10.length, bf16[1,64,4096]{2,1,0:T(8,128)(2,1)} %proj_in_hbm.1, bf16[1,64,4096]{2,1,0:T(8,128)(2,1)} %proj_out_hbm.1, f32[1,64,64]{2,1,0:T(8,128)} %out_factor_hbm.1, ...), custom_call_target="tpu_custom_call" | custom-call | tf_op jit(solution)/shard_map/pallas_call | solution.py:236
  15.4 0.6 %copy.11 = f32[8,128]{1,0:T(8,128)} copy(f32[8,128]{1,0:T(8,128)S(1)} %shard_map.82) | data formatting | bytes 8192

commit v5 on v2

--- a/solution.py
+++ b/solution.py
@@ -11,7 +11,7 @@
 F32 = jnp.float32
 BF16 = jnp.bfloat16
 NT = (((1,), (1,)), ((), ()))
-CHUNKS = 4
+CHUNKS = 1
 
 
 def split(x):
@@ -28,7 +28,7 @@
     m,
     inputs_hbm,
     cotangents_hbm,
-    lengths_hbm,
+    length,
     proj_in_hbm,
     proj_out_hbm,
     out_factor_hbm,
@@ -37,7 +37,6 @@
     out_ref,
     inputs,
     cotangents,
-    length,
     proj_in,
     proj_out,
     out_factor,
@@ -81,7 +80,6 @@
         )
     out_factor_load = load(small_sem.at[0], out_factor_hbm.at[0], out_factor)
     in_factor_load = load(small_sem.at[1], in_factor_hbm.at[0], in_factor)
-    length_load = load(small_sem.at[2], lengths_hbm, length)
     for c in range(CHUNKS):
         in_loads.append(
             (
@@ -123,9 +121,9 @@
         return total
 
     out_side = project(out_loads, proj_out, cotangents)
-    length_load.wait()
     slots = lax.broadcasted_iota(jnp.int32, (rank, tokens), 1)
     out_side = jnp.where(slots < length[0], out_side, 0.0)
+    pl.semaphore_wait(barrier, n - 1 + m - 1)
     in_side = project(in_loads, proj_in, inputs)
     out_twice = jnp.concatenate([out_side, out_side], axis=0).astype(BF16)
     in_twice = jnp.concatenate([in_side, in_side], axis=0).astype(BF16)
@@ -138,7 +136,6 @@
     both = jnp.dot(projected, weights[...], preferred_element_type=F32)
     own[...] = (both[:, :pair] + both[:, pair:]).astype(BF16)
 
-    pl.semaphore_wait(barrier, n - 1 + m - 1)
     sends = []
     for k in range(1, n):
         copy = pltpu.make_async_remote_copy(
@@ -194,7 +191,7 @@
 
 
 def body(n, m, *args):
-    inputs, _, lengths, proj_in, _, _, _, train = args
+    inputs, _, _, proj_in, _, _, _, train = args
     _, _, tokens, width = inputs.shape
     rank = proj_in.shape[1]
     count = train.shape[1]
@@ -204,12 +201,11 @@
     return pl.pallas_call(
         functools.partial(kernel, n, m),
         out_shape=jax.ShapeDtypeStruct((rows, count), F32),
-        in_specs=[hbm] * len(args),
+        in_specs=[hbm, hbm, pl.BlockSpec(memory_space=pltpu.SMEM)] + [hbm] * 5,
         out_specs=pl.BlockSpec(memory_space=pltpu.VMEM),
         scratch_shapes=[
             pltpu.VMEM((tokens, width), BF16),
             pltpu.VMEM((tokens, width), BF16),
-            pltpu.SMEM((1,), jnp.int32),
             pltpu.VMEM((rank, width), BF16),
             pltpu.VMEM((rank, width), BF16),
             pltpu.VMEM((rank, rank), F32),
@@ -229,7 +225,7 @@
             pltpu.SemaphoreType.DMA((m,)),
         ],
         compiler_params=pltpu.CompilerParams(
-            collective_id=0, has_side_effects=True, vmem_limit_bytes=63 * 1024 * 1024
+            collective_id=0, has_side_effects=True, vmem_limit_bytes=55212 * 1024
         ),
     )(*args)
 

time: 18.3 us -> 16.2 us (0.89)
  Pallas kernels: 16.2 us -> 14.8 us
  local copies, waits for them, and re-layouts: 1.28 us -> 0.6 us
    pallas_call x1, Pallas kernels: 16.2 us -> 14.8 us  [body(): pl.pallas_call(functools.partial(kernel, n, m), out_shape=jax.ShapeDtypeS...]
    unnamed x1, local copies, waits for them, and re-layouts: 1.28 us -> 0.6 us
where the time goes in v5:
time: 16.2 us; the launch traced here: 16.1 us
  Pallas kernels  14.8 us (91%)
  between operations  0.66 us (4%)
  local copies, waits for them, and re-layouts  0.6 us (4%)
    pallas_call x1, Pallas kernels, body(): pl.pallas_call(functools.partial(kernel, n, m), out_shape=jax.ShapeDtypeS...  14.8 us
    unnamed x1, local copies, waits for them, and re-layouts  0.6 us

profile of v5, /device:TPU:0, one launch (start us, length us, event | category | flops | bytes accessed | tf_op | source)
XLA Modules:
  0.0 16.1 jit_solution(1014456537453595773)
XLA Ops:
  0.7 14.8 %shard_map.82 = f32[8,128]{1,0:T(8,128)S(1)} custom-call(bf16[1,1,128,4096]{3,2,1,0:T(8,128)(2,1)} %inputs_hbm.1, bf16[1,1,128,4096]{3,2,1,0:T(8,128)(2,1)} %cotangents_hbm.1, s32[1]{0:T(128)S(6)} %copy.10.length, bf16[1,64,4096]{2,1,0:T(8,128)(2,1)} %proj_in_hbm.1, bf16[1,64,4096]{2,1,0:T(8,128)(2,1)} %proj_out_hbm.1, f32[1,64,64]{2,1,0:T(8,128)} %out_factor_hbm.1, ...), custom_call_target="tpu_custom_call" | custom-call | tf_op jit(solution)/shard_map/pallas_call | solution.py:201
  15.5 0.6 %copy.11 = f32[8,128]{1,0:T(8,128)} copy(f32[8,128]{1,0:T(8,128)S(1)} %shard_map.82) | data formatting | bytes 8192

commit v6 on v5

--- a/solution.py
+++ b/solution.py
@@ -90,12 +90,13 @@
     train_load = load(small_sem.at[3], train_hbm.at[0], train)
 
     barrier = pltpu.get_barrier_semaphore()
-    peers = [lax.rem(me + k, n) for k in range(1, n)]
+    core = lax.rem(me, 2)
+    sibling = me + 1 - 2 * core
+    peers = [lax.rem(me + 2 * k, n) for k in range(1, n // 2)]
     layers = [lax.rem(layer + k, m) for k in range(1, m)]
-    for peer in peers:
-        pl.semaphore_signal(barrier, inc=1, device_id=(peer, layer), device_id_type=MESH)
-    for other in layers:
-        pl.semaphore_signal(barrier, inc=1, device_id=(me, other), device_id_type=MESH)
+    greeted = [(peer, layer) for peer in peers + [sibling]] + [(me, other) for other in layers]
+    for device in greeted:
+        pl.semaphore_signal(barrier, inc=1, device_id=device, device_id_type=MESH)
 
     out_factor_load.wait()
     in_factor_load.wait()
@@ -123,7 +124,7 @@
     out_side = project(out_loads, proj_out, cotangents)
     slots = lax.broadcasted_iota(jnp.int32, (rank, tokens), 1)
     out_side = jnp.where(slots < length[0], out_side, 0.0)
-    pl.semaphore_wait(barrier, n - 1 + m - 1)
+    pl.semaphore_wait(barrier, len(greeted))
     in_side = project(in_loads, proj_in, inputs)
     out_twice = jnp.concatenate([out_side, out_side], axis=0).astype(BF16)
     in_twice = jnp.concatenate([in_side, in_side], axis=0).astype(BF16)
@@ -137,29 +138,40 @@
     own[...] = (both[:, :pair] + both[:, pair:]).astype(BF16)
 
     sends = []
-    for k in range(1, n):
+
+    def share(block, source, target):
         copy = pltpu.make_async_remote_copy(
-            src_ref=own,
-            dst_ref=gathered.at[me],
-            send_sem=send_sem.at[k],
-            recv_sem=recv_sem.at[me],
-            device_id=(peers[k - 1], layer),
+            src_ref=block,
+            dst_ref=gathered.at[source],
+            send_sem=send_sem.at[len(sends)],
+            recv_sem=recv_sem.at[source],
+            device_id=(target, layer),
             device_id_type=MESH,
         )
         copy.start()
         sends.append(copy)
-    gathered[me] = own[...]
-    train_load.wait()
-    for k in range(1, n):
-        source = lax.rem(me + n - k, n)
+
+    def arrive(source):
         pltpu.make_async_remote_copy(
             src_ref=own,
             dst_ref=gathered.at[source],
-            send_sem=send_sem.at[k],
+            send_sem=send_sem.at[0],
             recv_sem=recv_sem.at[source],
-            device_id=(peers[k - 1], layer),
+            device_id=(sibling, layer),
             device_id_type=MESH,
         ).wait_recv()
+
+    for peer in peers:
+        share(own, me, peer)
+    share(own, me, sibling)
+    gathered[me] = own[...]
+    for peer in peers:
+        arrive(peer)
+        share(gathered.at[peer], peer, sibling)
+    train_load.wait()
+    arrive(sibling)
+    for k in range(1, n // 2):
+        arrive(lax.rem(sibling + 2 * k, n))
 
     wide[...] = gathered[...].astype(F32).reshape(wide.shape)
     conditioned = jnp.concatenate(

time: 16.2 us -> 16.1 us (level)
  no operation moved by 1% of the time
where the time goes in v6:
time: 16.1 us; the launch traced here: 16 us
  Pallas kernels  14.7 us (91%)
  between operations  0.66 us (4%)
  local copies, waits for them, and re-layouts  0.6 us (4%)
    pallas_call x1, Pallas kernels, body(): pl.pallas_call(functools.partial(kernel, n, m), out_shape=jax.ShapeDtypeS...  14.7 us
    unnamed x1, local copies, waits for them, and re-layouts  0.6 us

profile of v6, /device:TPU:0, one launch (start us, length us, event | category | flops | bytes accessed | tf_op | source)
XLA Modules:
  0.0 16.0 jit_solution(445184302526969654)
XLA Ops:
  0.7 14.7 %shard_map.82 = f32[8,128]{1,0:T(8,128)S(1)} custom-call(bf16[1,1,128,4096]{3,2,1,0:T(8,128)(2,1)} %inputs_hbm.1, bf16[1,1,128,4096]{3,2,1,0:T(8,128)(2,1)} %cotangents_hbm.1, s32[1]{0:T(128)S(6)} %copy.10.length, bf16[1,64,4096]{2,1,0:T(8,128)(2,1)} %proj_in_hbm.1, bf16[1,64,4096]{2,1,0:T(8,128)(2,1)} %proj_out_hbm.1, f32[1,64,64]{2,1,0:T(8,128)} %out_factor_hbm.1, ...), custom_call_target="tpu_custom_call" | custom-call | tf_op jit(solution)/shard_map/pallas_call | solution.py:213
  15.4 0.6 %copy.11 = f32[8,128]{1,0:T(8,128)} copy(f32[8,128]{1,0:T(8,128)S(1)} %shard_map.82) | data formatting | bytes 8192

commit v7 on v6

--- a/solution.py
+++ b/solution.py
@@ -69,6 +69,8 @@
     def columns(c):
         return pl.ds(c * step, step)
 
+    out_factor_load = load(small_sem.at[0], out_factor_hbm.at[0], out_factor)
+    in_factor_load = load(small_sem.at[1], in_factor_hbm.at[0], in_factor)
     out_loads = []
     in_loads = []
     for c in range(CHUNKS):
@@ -78,8 +80,6 @@
                 load(load_sem.at[1, c], cotangents_hbm.at[0, 0, :, columns(c)], cotangents.at[:, columns(c)]),
             )
         )
-    out_factor_load = load(small_sem.at[0], out_factor_hbm.at[0], out_factor)
-    in_factor_load = load(small_sem.at[1], in_factor_hbm.at[0], in_factor)
     for c in range(CHUNKS):
         in_loads.append(
             (
@@ -87,7 +87,6 @@
                 load(load_sem.at[3, c], inputs_hbm.at[0, 0, :, columns(c)], inputs.at[:, columns(c)]),
             )
         )
-    train_load = load(small_sem.at[3], train_hbm.at[0], train)
 
     barrier = pltpu.get_barrier_semaphore()
     core = lax.rem(me, 2)
@@ -117,18 +116,19 @@
         for c in range(CHUNKS):
             for copy in loads[c]:
                 copy.wait()
-            term = dot_nt(proj[:, columns(c)], values[:, columns(c)])
+            term = dot_nt(values[:, columns(c)], proj[:, columns(c)])
             total = term if total is None else total + term
         return total
 
     out_side = project(out_loads, proj_out, cotangents)
-    slots = lax.broadcasted_iota(jnp.int32, (rank, tokens), 1)
-    out_side = jnp.where(slots < length[0], out_side, 0.0)
+    train_load = load(small_sem.at[3], train_hbm.at[0], train)
+    slots = lax.broadcasted_iota(jnp.int32, (tokens, rank), 0)
+    out_side = jnp.where(slots < length[0], out_side, 0.0).T
+    out_twice = jnp.concatenate([out_side, out_side], axis=0).astype(BF16)
     pl.semaphore_wait(barrier, len(greeted))
     in_side = project(in_loads, proj_in, inputs)
-    out_twice = jnp.concatenate([out_side, out_side], axis=0).astype(BF16)
-    in_twice = jnp.concatenate([in_side, in_side], axis=0).astype(BF16)
-    grads = dot_nt(out_twice, in_twice)
+    in_twice = jnp.concatenate([in_side, in_side], axis=1).astype(BF16)
+    grads = jnp.dot(out_twice, in_twice, preferred_element_type=F32)
     rows = lax.broadcasted_iota(jnp.int32, (pair, pair), 0) < rank
     cols = lax.broadcasted_iota(jnp.int32, (pair, pair), 1) < rank
     grads = jnp.where(rows == cols, grads, 0.0).astype(BF16)
@@ -150,6 +150,9 @@
         )
         copy.start()
         sends.append(copy)
+
+    def widen(block, source):
+        wide[pl.ds(pl.multiple_of(source * half, half), half), :] = block[...].astype(F32)
 
     def arrive(source):
         pltpu.make_async_remote_copy(
@@ -164,20 +167,21 @@
     for peer in peers:
         share(own, me, peer)
     share(own, me, sibling)
-    gathered[me] = own[...]
+    widen(own, me)
     for peer in peers:
         arrive(peer)
         share(gathered.at[peer], peer, sibling)
+        widen(gathered.at[peer], peer)
     train_load.wait()
-    arrive(sibling)
-    for k in range(1, n // 2):
-        arrive(lax.rem(sibling + 2 * k, n))
-
-    wide[...] = gathered[...].astype(F32).reshape(wide.shape)
+    for k in range(n // 2):
+        source = lax.rem(sibling + 2 * k, n)
+        arrive(source)
+        widen(gathered.at[source], source)
+
     conditioned = jnp.concatenate(
         [wide[pl.ds(j, n, stride=half), :] for j in range(half)], axis=1
     ).astype(BF16)
-    scores = dot_nt(conditioned, train[...])
+    scores = dot_nt(train[...], conditioned).T
     partial[...] = scores.reshape(partial.shape)
     layer_sends = []
     for k in range(1, m):

time: 16.1 us -> 16.4 us (1.019)
  Pallas kernels: 14.7 us -> 15 us
    pallas_call x1, Pallas kernels: 14.7 us -> 15 us  [body(): pl.pallas_call(functools.partial(kernel, n, m), out_shape=jax.ShapeDtypeS...]
where the time goes in v7:
time: 16.4 us; the launch traced here: 16.2 us
  Pallas kernels  15 us (91%)
  between operations  0.66 us (4%)
  local copies, waits for them, and re-layouts  0.6 us (4%)
    pallas_call x1, Pallas kernels, body(): pl.pallas_call(functools.partial(kernel, n, m), out_shape=jax.ShapeDtypeS...  15 us
    unnamed x1, local copies, waits for them, and re-layouts  0.6 us

profile of v7, /device:TPU:0, one launch (start us, length us, event | category | flops | bytes accessed | tf_op | source)
XLA Modules:
  0.0 16.2 jit_solution(17039382456797512325)
XLA Ops:
  0.7 15.0 %shard_map.82 = f32[8,128]{1,0:T(8,128)S(1)} custom-call(bf16[1,1,128,4096]{3,2,1,0:T(8,128)(2,1)} %inputs_hbm.1, bf16[1,1,128,4096]{3,2,1,0:T(8,128)(2,1)} %cotangents_hbm.1, s32[1]{0:T(128)S(6)} %copy.10.length, bf16[1,64,4096]{2,1,0:T(8,128)(2,1)} %proj_in_hbm.1, bf16[1,64,4096]{2,1,0:T(8,128)(2,1)} %proj_out_hbm.1, f32[1,64,64]{2,1,0:T(8,128)} %out_factor_hbm.1, ...), custom_call_target="tpu_custom_call" | custom-call | tf_op jit(solution)/shard_map/pallas_call | solution.py:217
  15.6 0.6 %copy.11 = f32[8,128]{1,0:T(8,128)} copy(f32[8,128]{1,0:T(8,128)S(1)} %shard_map.82) | data formatting | bytes 8192

commit v8 on v7

--- a/solution.py
+++ b/solution.py
@@ -69,10 +69,7 @@
     def columns(c):
         return pl.ds(c * step, step)
 
-    out_factor_load = load(small_sem.at[0], out_factor_hbm.at[0], out_factor)
-    in_factor_load = load(small_sem.at[1], in_factor_hbm.at[0], in_factor)
     out_loads = []
-    in_loads = []
     for c in range(CHUNKS):
         out_loads.append(
             (
@@ -80,14 +77,6 @@
                 load(load_sem.at[1, c], cotangents_hbm.at[0, 0, :, columns(c)], cotangents.at[:, columns(c)]),
             )
         )
-    for c in range(CHUNKS):
-        in_loads.append(
-            (
-                load(load_sem.at[2, c], proj_in_hbm.at[0, :, columns(c)], proj_in.at[:, columns(c)]),
-                load(load_sem.at[3, c], inputs_hbm.at[0, 0, :, columns(c)], inputs.at[:, columns(c)]),
-            )
-        )
-
     barrier = pltpu.get_barrier_semaphore()
     core = lax.rem(me, 2)
     sibling = me + 1 - 2 * core
@@ -96,6 +85,17 @@
     greeted = [(peer, layer) for peer in peers + [sibling]] + [(me, other) for other in layers]
     for device in greeted:
         pl.semaphore_signal(barrier, inc=1, device_id=device, device_id_type=MESH)
+
+    out_factor_load = load(small_sem.at[0], out_factor_hbm.at[0], out_factor)
+    in_factor_load = load(small_sem.at[1], in_factor_hbm.at[0], in_factor)
+    in_loads = []
+    for c in range(CHUNKS):
+        in_loads.append(
+            (
+                load(load_sem.at[2, c], proj_in_hbm.at[0, :, columns(c)], proj_in.at[:, columns(c)]),
+                load(load_sem.at[3, c], inputs_hbm.at[0, 0, :, columns(c)], inputs.at[:, columns(c)]),
+            )
+        )
 
     out_factor_load.wait()
     in_factor_load.wait()
@@ -125,7 +125,6 @@
     slots = lax.broadcasted_iota(jnp.int32, (tokens, rank), 0)
     out_side = jnp.where(slots < length[0], out_side, 0.0).T
     out_twice = jnp.concatenate([out_side, out_side], axis=0).astype(BF16)
-    pl.semaphore_wait(barrier, len(greeted))
     in_side = project(in_loads, proj_in, inputs)
     in_twice = jnp.concatenate([in_side, in_side], axis=1).astype(BF16)
     grads = jnp.dot(out_twice, in_twice, preferred_element_type=F32)
@@ -137,6 +136,7 @@
     both = jnp.dot(projected, weights[...], preferred_element_type=F32)
     own[...] = (both[:, :pair] + both[:, pair:]).astype(BF16)
 
+    pl.semaphore_wait(barrier, len(greeted))
     sends = []
 
     def share(block, source, target):

time: 16.4 us -> 16.4 us (level)
  no operation moved by 1% of the time
where the time goes in v8:
time: 16.4 us; the launch traced here: 16.2 us
  Pallas kernels  15 us (91%)
  between operations  0.66 us (4%)
  local copies, waits for them, and re-layouts  0.6 us (4%)
    pallas_call x1, Pallas kernels, body(): pl.pallas_call(functools.partial(kernel, n, m), out_shape=jax.ShapeDtypeS...  15 us
    unnamed x1, local copies, waits for them, and re-layouts  0.6 us

profile of v8, /device:TPU:0, one launch (start us, length us, event | category | flops | bytes accessed | tf_op | source)
XLA Modules:
  0.0 16.2 jit_solution(8290958119089175590)
XLA Ops:
  0.7 15.0 %shard_map.82 = f32[8,128]{1,0:T(8,128)S(1)} custom-call(bf16[1,1,128,4096]{3,2,1,0:T(8,128)(2,1)} %inputs_hbm.1, bf16[1,1,128,4096]{3,2,1,0:T(8,128)(2,1)} %cotangents_hbm.1, s32[1]{0:T(128)S(6)} %copy.10.length, bf16[1,64,4096]{2,1,0:T(8,128)(2,1)} %proj_in_hbm.1, bf16[1,64,4096]{2,1,0:T(8,128)(2,1)} %proj_out_hbm.1, f32[1,64,64]{2,1,0:T(8,128)} %out_factor_hbm.1, ...), custom_call_target="tpu_custom_call" | custom-call | tf_op jit(solution)/shard_map/pallas_call | solution.py:217
  15.6 0.6 %copy.11 = f32[8,128]{1,0:T(8,128)} copy(f32[8,128]{1,0:T(8,128)S(1)} %shard_map.82) | data formatting | bytes 8192

commit v9 on v4

--- a/solution.py
+++ b/solution.py
@@ -12,6 +12,7 @@
 BF16 = jnp.bfloat16
 NT = (((1,), (1,)), ((), ()))
 CHUNKS = 1
+STRIPS = 4
 
 
 def split(x):
@@ -71,7 +72,6 @@
         return pl.ds(c * step, step)
 
     out_loads = []
-    in_loads = []
     for c in range(CHUNKS):
         out_loads.append(
             (
@@ -79,8 +79,19 @@
                 load(load_sem.at[1, c], cotangents_hbm.at[0, 0, :, columns(c)], cotangents.at[:, columns(c)]),
             )
         )
+    barrier = pltpu.get_barrier_semaphore()
+    core = lax.rem(me, 2)
+    sibling = me + 1 - 2 * core
+    peers = [lax.rem(me + 2 * k, n) for k in range(1, n // 2)]
+    layers = [lax.rem(layer + k, m) for k in range(1, m)]
+    partners = [(sibling, layer)] + [(dp, other) for other in layers for dp in (me, sibling)]
+    greeted = [(peer, layer) for peer in peers] + partners
+    for device in greeted:
+        pl.semaphore_signal(barrier, inc=1, device_id=device, device_id_type=MESH)
+
     out_factor_load = load(small_sem.at[0], out_factor_hbm.at[0], out_factor)
     in_factor_load = load(small_sem.at[1], in_factor_hbm.at[0], in_factor)
+    in_loads = []
     for c in range(CHUNKS):
         in_loads.append(
             (
@@ -88,28 +99,7 @@
                 load(load_sem.at[3, c], inputs_hbm.at[0, 0, :, columns(c)], inputs.at[:, columns(c)]),
             )
         )
-    core = lax.rem(me, 2)
-    sibling = me + 1 - 2 * core
-    train_load = load(small_sem.at[2], train_hbm.at[0], train.at[core])
-
-    barrier = pltpu.get_barrier_semaphore()
-    peers = [lax.rem(me + 2 * k, n) for k in range(1, n // 2)]
-    layers = [lax.rem(layer + k, m) for k in range(1, m)]
-    partners = [(sibling, layer)] + [(dp, other) for other in layers for dp in (me, sibling)]
-    greeted = [(peer, layer) for peer in peers] + partners
-    for device in greeted:
-        pl.semaphore_signal(barrier, inc=1, device_id=device, device_id_type=MESH)
-
-    pl.semaphore_wait(barrier, len(greeted))
-    train_share = pltpu.make_async_remote_copy(
-        src_ref=train_hbm.at[0],
-        dst_ref=train.at[core],
-        send_sem=train_sem.at[0],
-        recv_sem=train_sem.at[1],
-        device_id=(sibling, layer),
-        device_id_type=MESH,
-    )
-    train_share.start()
+
     out_factor_load.wait()
     in_factor_load.wait()
     half = rank // 2
@@ -129,17 +119,32 @@
         for c in range(CHUNKS):
             for copy in loads[c]:
                 copy.wait()
-            term = dot_nt(proj[:, columns(c)], values[:, columns(c)])
+            term = dot_nt(values[:, columns(c)], proj[:, columns(c)])
             total = term if total is None else total + term
         return total
 
     out_side = project(out_loads, proj_out, cotangents)
-    slots = lax.broadcasted_iota(jnp.int32, (rank, tokens), 1)
-    out_side = jnp.where(slots < length[0], out_side, 0.0)
+    slots = lax.broadcasted_iota(jnp.int32, (tokens, rank), 0)
+    out_side = jnp.where(slots < length[0], out_side, 0.0).T
+    out_twice = jnp.concatenate([out_side, out_side], axis=0).astype(BF16)
+    pl.semaphore_wait(barrier, len(greeted))
+    train_shares = []
+    strip = train.shape[1] // STRIPS
+    for c in range(STRIPS):
+        copy = pltpu.make_async_remote_copy(
+            src_ref=train_hbm.at[0, pl.ds(c * strip, strip), :],
+            dst_ref=train.at[core, pl.ds(c * strip, strip), :],
+            send_sem=train_sem.at[0, c],
+            recv_sem=train_sem.at[1, c],
+            device_id=(sibling, layer),
+            device_id_type=MESH,
+        )
+        copy.start()
+        train_shares.append(copy)
+    train_load = load(small_sem.at[2], train_hbm.at[0], train.at[core])
     in_side = project(in_loads, proj_in, inputs)
-    out_twice = jnp.concatenate([out_side, out_side], axis=0).astype(BF16)
-    in_twice = jnp.concatenate([in_side, in_side], axis=0).astype(BF16)
-    grads = dot_nt(out_twice, in_twice)
+    in_twice = jnp.concatenate([in_side, in_side], axis=1).astype(BF16)
+    grads = jnp.dot(out_twice, in_twice, preferred_element_type=F32)
     rows = lax.broadcasted_iota(jnp.int32, (pair, pair), 0) < rank
     cols = lax.broadcasted_iota(jnp.int32, (pair, pair), 1) < rank
     grads = jnp.where(rows == cols, grads, 0.0).astype(BF16)
@@ -161,16 +166,14 @@
         )
         copy.start()
         sends.append(copy)
-    gathered[place] = own[...]
+
+    def widen(block, index):
+        wide[pl.ds(pl.multiple_of(index * half, half), half), :] = block[...].astype(F32)
+
+    widen(own, place)
     train_load.wait()
-    pltpu.make_async_remote_copy(
-        src_ref=train_hbm.at[0],
-        dst_ref=train.at[1 - core],
-        send_sem=train_sem.at[0],
-        recv_sem=train_sem.at[1],
-        device_id=(sibling, layer),
-        device_id_type=MESH,
-    ).wait_recv()
+    for copy in train_shares:
+        copy.wait_recv()
     for k, peer in enumerate(peers):
         source = peer // 2
         pltpu.make_async_remote_copy(
@@ -181,12 +184,11 @@
             device_id=(peer, layer),
             device_id_type=MESH,
         ).wait_recv()
-
-    wide[...] = gathered[...].astype(F32).reshape(wide.shape)
+        widen(gathered.at[source], source)
     conditioned = jnp.concatenate(
         [wide[pl.ds(j, n // 2, stride=half), :] for j in range(half)], axis=1
     ).astype(BF16)
-    scores = dot_nt(conditioned, train[...].reshape(2 * train.shape[1], train.shape[2]))
+    scores = dot_nt(train[...].reshape(2 * train.shape[1], train.shape[2]), conditioned).T
     _, _, rows, count = partial.shape
     for other in range(m):
         for c in range(2):
@@ -204,7 +206,8 @@
         copy.start()
         results.append(copy)
     arrived[layer, core] = partial[layer, core]
-    train_share.wait_send()
+    for copy in train_shares:
+        copy.wait_send()
     for copy in sends:
         copy.wait_send()
     for k, (dp, other) in enumerate(partners):
@@ -254,7 +257,7 @@
             pltpu.VMEM((m, 2, rows // 2, count), F32),
             pltpu.SemaphoreType.DMA((4, CHUNKS)),
             pltpu.SemaphoreType.DMA((3,)),
-            pltpu.SemaphoreType.DMA((2,)),
+            pltpu.SemaphoreType.DMA((2, STRIPS)),
             pltpu.SemaphoreType.DMA((n // 2,)),
             pltpu.SemaphoreType.DMA((n // 2,)),
             pltpu.SemaphoreType.DMA((2 * m,)),

time: 16.2 us -> 16.6 us (1.025)
  Pallas kernels: 14.8 us -> 15.2 us
    pallas_call x1, Pallas kernels: 14.8 us -> 15.2 us  [body(): pl.pallas_call(functools.partial(kernel, n, m), out_shape=jax.ShapeDtypeS...]
where the time goes in v9:
time: 16.6 us; the launch traced here: 16.4 us
  Pallas kernels  15.2 us (92%)
  between operations  0.66 us (4%)
  local copies, waits for them, and re-layouts  0.6 us (4%)
    pallas_call x1, Pallas kernels, body(): pl.pallas_call(functools.partial(kernel, n, m), out_shape=jax.ShapeDtypeS...  15.2 us
    unnamed x1, local copies, waits for them, and re-layouts  0.6 us

profile of v9, /device:TPU:0, one launch (start us, length us, event | category | flops | bytes accessed | tf_op | source)
XLA Modules:
  0.0 16.4 jit_solution(3257701642968459538)
XLA Ops:
  0.7 15.2 %shard_map.82 = f32[8,128]{1,0:T(8,128)S(1)} custom-call(bf16[1,1,128,4096]{3,2,1,0:T(8,128)(2,1)} %inputs_hbm.1, bf16[1,1,128,4096]{3,2,1,0:T(8,128)(2,1)} %cotangents_hbm.1, s32[1]{0:T(128)S(6)} %copy.10.length, bf16[1,64,4096]{2,1,0:T(8,128)(2,1)} %proj_in_hbm.1, bf16[1,64,4096]{2,1,0:T(8,128)(2,1)} %proj_out_hbm.1, f32[1,64,64]{2,1,0:T(8,128)} %out_factor_hbm.1, ...), custom_call_target="tpu_custom_call" | custom-call | tf_op jit(solution)/shard_map/pallas_call | solution.py:239
  15.8 0.6 %copy.11 = f32[8,128]{1,0:T(8,128)} copy(f32[8,128]{1,0:T(8,128)S(1)} %shard_map.82) | data formatting | bytes 8192

commit v10 on v8

--- a/solution.py
+++ b/solution.py
@@ -85,6 +85,12 @@
     greeted = [(peer, layer) for peer in peers + [sibling]] + [(me, other) for other in layers]
     for device in greeted:
         pl.semaphore_signal(barrier, inc=1, device_id=device, device_id_type=MESH)
+    place = me // 2
+
+    @pl.when(place == 0)
+    def _():
+        for k in range(1, n // 2):
+            pl.semaphore_signal(barrier, inc=1, device_id=(sibling + 2 * k, layer), device_id_type=MESH)
 
     out_factor_load = load(small_sem.at[0], out_factor_hbm.at[0], out_factor)
     in_factor_load = load(small_sem.at[1], in_factor_hbm.at[0], in_factor)
@@ -136,20 +142,20 @@
     both = jnp.dot(projected, weights[...], preferred_element_type=F32)
     own[...] = (both[:, :pair] + both[:, pair:]).astype(BF16)
 
-    pl.semaphore_wait(barrier, len(greeted))
+    pl.semaphore_wait(barrier, len(greeted) + (place + n // 2 - 1) // (n // 2))
     sends = []
 
-    def share(block, source, target):
+    def share(block, source, target, sem):
         copy = pltpu.make_async_remote_copy(
             src_ref=block,
             dst_ref=gathered.at[source],
-            send_sem=send_sem.at[len(sends)],
+            send_sem=send_sem.at[sem],
             recv_sem=recv_sem.at[source],
             device_id=(target, layer),
             device_id_type=MESH,
         )
         copy.start()
-        sends.append(copy)
+        return copy
 
     def widen(block, source):
         wide[pl.ds(pl.multiple_of(source * half, half), half), :] = block[...].astype(F32)
@@ -164,13 +170,21 @@
             device_id_type=MESH,
         ).wait_recv()
 
-    for peer in peers:
-        share(own, me, peer)
-    share(own, me, sibling)
+    @pl.when(place > 0)
+    def _():
+        share(own, me, 1 - core, 0)
+
+    for k, peer in enumerate(peers):
+        sends.append(share(own, me, peer, 1 + k))
+    sends.append(share(own, me, sibling, n // 2))
     widen(own, me)
-    for peer in peers:
+    for k, peer in enumerate(peers):
         arrive(peer)
-        share(gathered.at[peer], peer, sibling)
+
+        @pl.when(place > 0)
+        def _():
+            share(gathered.at[peer], peer, sibling, n // 2 + 1 + k)
+
         widen(gathered.at[peer], peer)
     train_load.wait()
     for k in range(n // 2):
@@ -198,6 +212,19 @@
     total = partial[layer]
     for copy in sends:
         copy.wait_send()
+
+    @pl.when(place > 0)
+    def _():
+        for sem in [0] + list(range(n // 2 + 1, n)):
+            pltpu.make_async_remote_copy(
+                src_ref=own,
+                dst_ref=gathered.at[me],
+                send_sem=send_sem.at[sem],
+                recv_sem=recv_sem.at[me],
+                device_id=(sibling, layer),
+                device_id_type=MESH,
+            ).wait_send()
+
     for k in range(1, m):
         layer_sends[k - 1].wait_recv()
         total = total + arrived[k]

time: 16.4 us -> 16.5 us (level)
  no operation moved by 1% of the time
where the time goes in v10:
time: 16.5 us; the launch traced here: 16.3 us
  Pallas kernels  15.1 us (92%)
  between operations  0.66 us (4%)
  local copies, waits for them, and re-layouts  0.6 us (4%)
    pallas_call x1, Pallas kernels, body(): pl.pallas_call(functools.partial(kernel, n, m), out_shape=jax.ShapeDtypeS...  15.1 us
    unnamed x1, local copies, waits for them, and re-layouts  0.6 us

profile of v10, /device:TPU:0, one launch (start us, length us, event | category | flops | bytes accessed | tf_op | source)
XLA Modules:
  0.0 16.3 jit_solution(1114088794091200903)
XLA Ops:
  0.7 15.1 %shard_map.82 = f32[8,128]{1,0:T(8,128)S(1)} custom-call(bf16[1,1,128,4096]{3,2,1,0:T(8,128)(2,1)} %inputs_hbm.1, bf16[1,1,128,4096]{3,2,1,0:T(8,128)(2,1)} %cotangents_hbm.1, s32[1]{0:T(128)S(6)} %copy.10.length, bf16[1,64,4096]{2,1,0:T(8,128)(2,1)} %proj_in_hbm.1, bf16[1,64,4096]{2,1,0:T(8,128)(2,1)} %proj_out_hbm.1, f32[1,64,64]{2,1,0:T(8,128)} %out_factor_hbm.1, ...), custom_call_target="tpu_custom_call" | custom-call | tf_op jit(solution)/shard_map/pallas_call | solution.py:244
  15.7 0.6 %copy.11 = f32[8,128]{1,0:T(8,128)} copy(f32[8,128]{1,0:T(8,128)S(1)} %shard_map.82) | data formatting | bytes 8192

commit v11 on v6

--- a/solution.py
+++ b/solution.py
@@ -11,7 +11,7 @@
 F32 = jnp.float32
 BF16 = jnp.bfloat16
 NT = (((1,), (1,)), ((), ()))
-CHUNKS = 1
+CHUNKS = 2
 
 
 def split(x):

time: 16.1 us -> 16.5 us (1.025)
  Pallas kernels: 14.7 us -> 15.1 us
    pallas_call x1, Pallas kernels: 14.7 us -> 15.1 us  [body(): pl.pallas_call(functools.partial(kernel, n, m), out_shape=jax.ShapeDtypeS...]
where the time goes in v11:
time: 16.5 us; the launch traced here: 16.3 us
  Pallas kernels  15.1 us (92%)
  between operations  0.66 us (4%)
  local copies, waits for them, and re-layouts  0.6 us (4%)
    pallas_call x1, Pallas kernels, body(): pl.pallas_call(functools.partial(kernel, n, m), out_shape=jax.ShapeDtypeS...  15.1 us
    unnamed x1, local copies, waits for them, and re-layouts  0.6 us

profile of v11, /device:TPU:0, one launch (start us, length us, event | category | flops | bytes accessed | tf_op | source)
XLA Modules:
  0.0 16.3 jit_solution(14594189229593003734)
XLA Ops:
  0.7 15.1 %shard_map.82 = f32[8,128]{1,0:T(8,128)S(1)} custom-call(bf16[1,1,128,4096]{3,2,1,0:T(8,128)(2,1)} %inputs_hbm.1, bf16[1,1,128,4096]{3,2,1,0:T(8,128)(2,1)} %cotangents_hbm.1, s32[1]{0:T(128)S(6)} %copy.10.length, bf16[1,64,4096]{2,1,0:T(8,128)(2,1)} %proj_in_hbm.1, bf16[1,64,4096]{2,1,0:T(8,128)(2,1)} %proj_out_hbm.1, f32[1,64,64]{2,1,0:T(8,128)} %out_factor_hbm.1, ...), custom_call_target="tpu_custom_call" | custom-call | tf_op jit(solution)/shard_map/pallas_call | solution.py:213
  15.7 0.6 %copy.11 = f32[8,128]{1,0:T(8,128)} copy(f32[8,128]{1,0:T(8,128)S(1)} %shard_map.82) | data formatting | bytes 8192
